TPU v7x, 128 devices: a whole 4x4x4 slice. The times are simulated.
128 devices in a mesh: had: 8 (over z, core), blk: 16 (over x, y).
Axes of the slice: x: 4, y: 4, z: 4, core: 2. Of those that a mesh axis runs over, the one named last changes fastest.
Arguments:
- panel: bfloat16 [262144, 512], P(('had', 'blk')), may hold values from -100 to 100
- signs: int32 [262144], P(('had', 'blk')), may hold values from 0 to 1
- sample_rows: int32 [16, 2048], P('blk'), may hold values from 0 to 16383
Outputs:
- q_panel: bfloat16 [262144, 512], P(('had', 'blk'))
- r_sketch: float32 [512, 512], replicated
- r_gram: float32 [512, 512], replicated
All inputs are finite; a program needn't handle non-finite values.
Results may differ from a plain program's by a relative error of at most 0.0075.
The roundings to bfloat16 on the way count: a program that leaves them out, or rounds other values in their place, can miss the bound.
Values sent between devices are 32-bit elements; how exact they have to be, the bound alone decides.
No kernel may reach another device: no remote copies, remote signals or barrier semaphores. Data moves between devices by JAX's collectives and lax.ppermute only.
A program may use at most 448 MiB of HBM per device.

v0:
```python
import math

import jax
import jax.numpy as jnp
from jax import lax
from jax.sharding import PartitionSpec as P

LH = 32


def bit_parity(value):
    counted = jnp.zeros_like(value)
    for shift_count in range(16):
        counted = counted + jnp.bitwise_and(jnp.right_shift(value, shift_count), 1)
    return counted % 2


def hadamard(order):
    first = lax.broadcasted_iota(jnp.int32, (order, order), 0)
    second = lax.broadcasted_iota(jnp.int32, (order, order), 1)
    parity = bit_parity(jnp.bitwise_and(first, second))
    return (1 - 2 * parity).astype(jnp.float32)


def upper_factor(matrix):
    return jnp.linalg.cholesky(matrix).T


def lower_inverse(lower):
    order = lower.shape[0]
    inverse = (1.0 / jnp.diagonal(lower)).reshape(order, 1, 1)
    width = 1
    while width < order:
        count = order // (2 * width)
        tiles = lower.reshape(count, 2 * width, count, 2 * width)
        diag_tiles = jnp.moveaxis(jnp.diagonal(tiles, axis1=0, axis2=2), -1, 0)
        corner = diag_tiles[:, width:, :width]
        first_inv = inverse[0::2]
        second_inv = inverse[1::2]
        partial_value = jnp.einsum(
            "ajk,akl->ajl", corner, first_inv, precision=lax.Precision.HIGHEST
        )
        lower_left = -jnp.einsum(
            "aij,ajl->ail", second_inv, partial_value, precision=lax.Precision.HIGHEST
        )
        zero_tile = jnp.zeros_like(corner)
        top_half = jnp.concatenate([first_inv, zero_tile], axis=2)
        bottom_half = jnp.concatenate([lower_left, second_inv], axis=2)
        inverse = jnp.concatenate([top_half, bottom_half], axis=1)
        width = width * 2
    return inverse[0]


def inverse_upper(factor):
    return lower_inverse(factor.T).T


def on_device(panel, signs, sample_rows):
    n_had = lax.axis_size("had")
    n_blk = lax.axis_size("blk")
    my_group = lax.axis_index("had")
    rows_dev, columns = panel.shape
    sketch_count = sample_rows.shape[1]
    groups = rows_dev // LH
    flipped = jnp.where(signs[:, None] == 1, -panel, panel)
    inner = hadamard(LH).astype(jnp.bfloat16)
    mixed = jnp.einsum(
        "ml,glk->gmk",
        inner,
        flipped.reshape(groups, LH, columns),
        preferred_element_type=jnp.float32,
    )
    mixed = mixed.reshape(rows_dev, columns)
    picks = sample_rows[0]
    owners = picks // rows_dev
    offsets = picks % rows_dev
    factor = 1.0 / math.sqrt(n_had * LH * sketch_count * n_blk)
    parity = bit_parity(jnp.bitwise_and(owners, my_group))
    weights = (1 - 2 * parity).astype(jnp.float32) * factor
    partial_sketch = jnp.take(mixed, offsets, axis=0) * weights[:, None]
    sketch = lax.psum(partial_sketch, ("had", "blk"))
    sketch_gram = jnp.dot(
        sketch.T, sketch, precision=lax.Precision.HIGHEST, preferred_element_type=jnp.float32
    )
    r_sketch = upper_factor(sketch_gram)
    sketch_inverse = inverse_upper(r_sketch).astype(jnp.bfloat16)
    whitened = jnp.dot(panel, sketch_inverse, preferred_element_type=jnp.float32).astype(
        jnp.bfloat16
    )
    partial_gram = jnp.einsum("rk,rj->kj", whitened, whitened, preferred_element_type=jnp.float32)
    summed = lax.psum(partial_gram, ("had", "blk"))
    gram_matrix = summed / (rows_dev * n_had * n_blk)
    r_gram = upper_factor(gram_matrix)
    gram_inverse = inverse_upper(r_gram).astype(jnp.bfloat16)
    q_panel = jnp.dot(whitened, gram_inverse, preferred_element_type=jnp.float32).astype(
        jnp.bfloat16
    )
    return (q_panel, r_sketch, r_gram)


def solution(mesh):
    placed = (P(("had", "blk"), None), P(("had", "blk")), P("blk", None))
    return jax.shard_map(
        on_device,
        mesh=mesh,
        in_specs=placed,
        out_specs=(P(("had", "blk"), None), P(), P()),
        check_vma=False,
    )
```

profile of v0, /device:TPU:1, one launch (start us, length us, event | category | flops | bytes accessed | tf_op | source)
XLA Modules:
  0.0 1254.7 jit_solution(11039515458677484619)
XLA Ops:
  12.5 11.7 gather_fusion
  28.4 157.2 %all-reduce.22.cloned.1.call-done = f32[2048,512]{1,0:T(8,128)} async-done(((f32[2048,512]{1,0:T(8,128)}), f32[2048,512]{1,0:T(8,128)}) %all-reduce.22.cloned.1.call-update) | async-done | bytes 4194320 | tf_op jit(solution)/shard_map/psum | solution.py:81
  185.6 10.5 fusion.185
  197.7 11.7 cholesky.286
  209.6 9.8 custom-call.59
  222.0 11.7 cholesky.305
  233.7 10.2 custom-call.60
  245.5 11.7 cholesky.326
  257.2 9.8 custom-call.61
  268.5 11.7 cholesky.343
  290.1 68.4 %reshape.325 = f32[256,2,256,2]{3,2,1,0:T(8,128)} reshape(f32[512,512]{1,0:T(8,128)S(1)} %select_select_fusion.1) | data formatting | bytes 2097152 | tf_op jit(solution)/shard_map/reshape | solution.py:35
  358.4 35.9 %reshape.326 = f32[128,4,128,4]{3,2,1,0:T(8,128)} reshape(f32[512,512]{1,0:T(8,128)S(1)} %select_select_fusion.1) | data formatting | bytes 2097152 | tf_op jit(solution)/shard_map/reshape | solution.py:35
  394.4 11.0 reshape.327
  418.8 107.3 %copy.213 = f32[256,2,256,2]{3,1,2,0:T(2,128)} copy(f32[256,2,256,2]{3,2,1,0:T(8,128)} %reshape.325) | data formatting | bytes 2097152 | tf_op jit(solution)/shard_map/reshape | solution.py:35
  529.4 38.0 %copy.215 = f32[128,4,128,4]{3,1,2,0:T(4,128)} copy(f32[128,4,128,4]{3,2,1,0:T(8,128)} %reshape.326) | data formatting | bytes 2097152 | tf_op jit(solution)/shard_map/reshape | solution.py:35
  571.6 20.5 %copy.217 = f32[64,8,64,8]{3,1,2,0:T(8,128)} copy(f32[64,8,64,8]{3,2,1,0:T(8,128)} %reshape.327) | data formatting | bytes 2097152 | tf_op jit(solution)/shard_map/reshape | solution.py:35
  599.8 14.2 %copy.219 = f32[32,16,32,16]{3,1,2,0:T(8,128)} copy(f32[32,16,32,16]{3,2,1,0:T(8,128)} %reshape.328) | data formatting | bytes 2097152 | tf_op jit(solution)/shard_map/reshape | solution.py:35
  649.1 144.4 %all-reduce.24.cloned.1.call-done = f32[512,512]{0,1:T(8,128)} async-done(((f32[512,512]{0,1:T(8,128)}), f32[512,512]{0,1:T(8,128)}) %all-reduce.24.cloned.1.call-update) | async-done | bytes 1048592 | tf_op jit(solution)/shard_map/psum | solution.py:91
  795.5 11.7 cholesky.358
  807.4 10.0 custom-call.62
  818.0 11.7 cholesky.377
  829.8 9.8 custom-call.63
  840.3 11.7 cholesky.398
  852.0 10.3 custom-call.64
  862.9 11.7 cholesky.415
  885.0 68.4 %reshape.336 = f32[256,2,256,2]{3,2,1,0:T(8,128)} reshape(f32[512,512]{1,0:T(8,128)S(1)} %select_select_fusion) | data formatting | bytes 2097152 | tf_op jit(solution)/shard_map/reshape | solution.py:35
  953.4 35.9 %reshape.337 = f32[128,4,128,4]{3,2,1,0:T(8,128)} reshape(f32[512,512]{1,0:T(8,128)S(1)} %select_select_fusion) | data formatting | bytes 2097152 | tf_op jit(solution)/shard_map/reshape | solution.py:35
  989.3 11.0 reshape.338
  1014.1 107.3 %copy.212 = f32[256,2,256,2]{3,1,2,0:T(2,128)} copy(f32[256,2,256,2]{3,2,1,0:T(8,128)} %reshape.336) | data formatting | bytes 2097152 | tf_op jit(solution)/shard_map/reshape | solution.py:35
  1124.7 37.8 %copy.214 = f32[128,4,128,4]{3,1,2,0:T(4,128)} copy(f32[128,4,128,4]{3,2,1,0:T(8,128)} %reshape.337) | data formatting | bytes 2097152 | tf_op jit(solution)/shard_map/reshape | solution.py:35
  1166.7 20.3 %copy.216 = f32[64,8,64,8]{3,1,2,0:T(8,128)} copy(f32[64,8,64,8]{3,2,1,0:T(8,128)} %reshape.338) | data formatting | bytes 2097152 | tf_op jit(solution)/shard_map/reshape | solution.py:35
  1194.8 14.2 %copy.218 = f32[32,16,32,16]{3,1,2,0:T(8,128)} copy(f32[32,16,32,16]{3,2,1,0:T(8,128)} %reshape.339) | data formatting | bytes 2097152 | tf_op jit(solution)/shard_map/reshape | solution.py:35
  (236 shorter events, 166.2 us)
Async XLA Ops:
  7.2 178.5 %all-reduce.22.cloned.1.call-start = ((), (), s32[]{:S(2)}) async-start(), calls=%async_computation | async-start | bytes 8388608 | tf_op jit(solution)/shard_map/psum | solution.py:81
  9.7 2.7 copy-start.22
  28.2 765.3 %all-reduce.24.cloned.1.call-start = ((), (), s32[]{:S(2)}) async-start(), calls=%async_computation.1 | async-start | bytes 2097152 | tf_op jit(solution)/shard_map/psum | solution.py:91
  28.2 539.2 %copy-start.4 = (s32[128]{0:T(128)}, s32[128]{0:T(128)S(1)}, u32[]{:S(2)}) copy-start(s32[128]{0:T(128)S(1)} %or_bitcast_fusion.6) | copy-start | bytes 1540
  28.3 563.8 %copy-start.6 = (s32[64]{0:T(128)}, s32[64]{0:T(128)S(1)}, u32[]{:S(2)}) copy-start(s32[64]{0:T(128)S(1)} %or_bitcast_fusion.5) | copy-start | bytes 772
  28.3 585.7 %copy-start.15 = (s32[32]{0:T(128)}, s32[32]{0:T(128)S(1)}, u32[]{:S(2)}) copy-start(s32[32]{0:T(128)S(1)} %or_bitcast_fusion.4) | copy-start | bytes 388
  28.3 596.0 %copy-start.17 = (s32[16]{0:T(128)}, s32[16]{0:T(128)S(1)}, u32[]{:S(2)}) copy-start(s32[16]{0:T(128)S(1)} %or_bitcast_fusion.3) | copy-start | bytes 196
  28.3 602.9 %copy-start.20 = (s32[8]{0:T(128)}, s32[8]{0:T(128)S(1)}, u32[]{:S(2)}) copy-start(s32[8]{0:T(128)S(1)} %or_bitcast_fusion.2) | copy-start | bytes 100
  28.4 607.0 %copy-start.23 = (s32[4]{0:T(128)}, s32[4]{0:T(128)S(1)}, u32[]{:S(2)}) copy-start(s32[4]{0:T(128)S(1)} %or_bitcast_fusion.1) | copy-start | bytes 52
  28.4 497.7 %copy-start.2 = (s32[256,1]{0,1:T(1,128)}, s32[256,1]{0,1:T(1,128)S(1)}, u32[]{:S(2)}) copy-start(s32[256,1]{0,1:T(1,128)S(1)} %shift-left_or_fusion.1) | copy-start | bytes 3076
  28.4 256.5 %copy-start = (s32[512,1]{0,1:T(1,128)}, s32[512,1]{0,1:T(1,128)S(1)}, u32[]{:S(2)}) copy-start(s32[512,1]{0,1:T(1,128)S(1)} %shift-left_or_fusion) | copy-start | bytes 6148
  196.8 1.0 copy-start.10
  644.0 1.3 copy-start.25
  793.5 1.8 copy-start.8
  795.5 84.6 %copy-start.1 = (s32[512,1]{0,1:T(1,128)S(1)}, s32[512,1]{0,1:T(1,128)}, u32[]{:S(2)}) copy-start(s32[512,1]{0,1:T(1,128)} %copy-done) | copy-start | bytes 6148
  1014.1 107.3 %copy-start.3 = (s32[256,1]{0,1:T(1,128)S(1)}, s32[256,1]{0,1:T(1,128)}, u32[]{:S(2)}) copy-start(s32[256,1]{0,1:T(1,128)} %copy-done.2) | copy-start | bytes 3076
  1124.7 37.8 %copy-start.5 = (s32[128]{0:T(128)S(1)}, s32[128]{0:T(128)}, u32[]{:S(2)}) copy-start(s32[128]{0:T(128)} %copy-done.4) | copy-start | bytes 1540
  1166.7 20.3 %copy-start.7 = (s32[64]{0:T(128)S(1)}, s32[64]{0:T(128)}, u32[]{:S(2)}) copy-start(s32[64]{0:T(128)} %copy-done.6) | copy-start | bytes 772
  1194.8 14.2 %copy-start.16 = (s32[32]{0:T(128)S(1)}, s32[32]{0:T(128)}, u32[]{:S(2)}) copy-start(s32[32]{0:T(128)} %copy-done.15) | copy-start | bytes 388
  1213.8 5.4 copy-start.18
  1219.3 7.0 copy-start.21
  1222.9 0.7 copy-start.11
  1226.3 6.7 copy-start.24
  1230.2 0.7 copy-start.12
  1232.9 5.3 copy-start.9
  1236.9 0.7 copy-start.13
  1238.4 1.0 copy-start.14
  1238.4 1.7 copy-start.19
Sparse Core Ops, SparseCore 0:
  28.3 157.3 all-reduce.21
  647.8 145.6 all-reduce.23
where the time goes:
time: 1260 us; the launch traced here: 1250 us
  local copies, waits for them, and re-layouts  708 us (56%)
  waiting for transfers between devices  302 us (24%)
  other arithmetic  175 us (14%)
  matrix products  49 us (4%)
  between operations  21 us (2%)
    reshape x32, local copies, waits for them, and re-layouts, lower_inverse(): tiles = lower.reshape(count, 2 * width, count, 2 * width)  635 us
    another operation x29, other arithmetic, upper_factor(): return jnp.linalg.cholesky(matrix).T  158 us
    psum x1, waiting for transfers between devices, on_device(): sketch = lax.psum(partial_sketch, ('had', 'blk'))  157 us
    psum x1, waiting for transfers between devices, on_device(): summed = lax.psum(partial_gram, ('had', 'blk'))  144 us
    gather x16, local copies, waits for them, and re-layouts, lower_inverse(): diag_tiles = jnp.moveaxis(jnp.diagonal(tiles, axis1=0, axis2=2), -1, 0)  40.2 us
  transfers between devices with their start and end apart: 2, of which 2 were waited for; matrix products, arithmetic and copies ran while one was open for 0% of the time, Pallas kernels for 0%

commit v1 on v0

v1 whole, which is shorter than its diff:
```python
import functools

import jax
import jax.numpy as jnp
from jax import lax
from jax.experimental import pallas as pl
from jax.experimental.pallas import tpu as pltpu
from jax.sharding import Mesh, PartitionSpec as P

LH = 32
NB = 64
GB = 128
AXES = ("z", "c", "x", "y")
CHIPS = ("z", "x", "y")
HIGHEST = lax.Precision.HIGHEST
VMEM = pl.BlockSpec(memory_space=pltpu.VMEM)
PARAMS = pltpu.CompilerParams(vmem_limit_bytes=48 * 1024 * 1024)


def dot(first, second, first_dim=1, second_dim=0, precision=None):
    return lax.dot_general(
        first,
        second,
        (((first_dim,), (second_dim,)), ((), ())),
        precision=precision,
        preferred_element_type=jnp.float32,
    )


def upper_blocks(columns):
    count = columns // GB
    return [(i, j) for i in range(count) for j in range(i, count)]


def sketch_kernel(codes_ref, signs_ref, panel_ref, out_ref):
    rows = panel_ref.shape[0]
    lane = lax.broadcasted_iota(jnp.int32, (128, 128), 1)
    inner_lane = jnp.bitwise_and(lane, LH - 1)
    group_lane = lane // LH
    flips = (1 - 2 * signs_ref[...]).astype(jnp.float32)
    for chunk in range(codes_ref.shape[1] // 256):
        strips = []
        for part in range(2):
            start = chunk * 256 + part * 128
            code = jnp.broadcast_to(codes_ref[:, start : start + 128], (128, 128)).T
            bits = jnp.bitwise_and(jnp.bitwise_and(code, LH - 1), inner_lane)
            bits = jnp.bitwise_xor(bits, jnp.right_shift(bits, 4))
            bits = jnp.bitwise_xor(bits, jnp.right_shift(bits, 2))
            bits = jnp.bitwise_xor(bits, jnp.right_shift(bits, 1))
            bits = jnp.bitwise_xor(bits, jnp.right_shift(code, 16))
            values = (1 - 2 * jnp.bitwise_and(bits, 1)).astype(jnp.float32)
            group = jnp.bitwise_and(jnp.right_shift(code, 5), 63) - group_lane
            strips.append((values, group))
        tiles = []
        for tile in range(rows // 128):
            flip = flips[:, tile * 128 : tile * 128 + 128]
            tiles.append(
                jnp.concatenate(
                    [jnp.where(group == 4 * tile, values * flip, 0.0).astype(jnp.bfloat16)
                     for values, group in strips],
                    axis=0,
                )
            )
        chosen = jnp.concatenate(tiles, axis=1)
        out_ref[chunk * 256 : chunk * 256 + 256, :] = dot(chosen, panel_ref[...])


def sketch_rows(codes, signs, panel):
    return pl.pallas_call(
        sketch_kernel,
        out_shape=jax.ShapeDtypeStruct((codes.shape[1], panel.shape[1]), jnp.float32),
        in_specs=[VMEM] * 3,
        out_specs=VMEM,
        compiler_params=PARAMS,
        name="sketch_rows",
    )(codes, signs, panel)


def pack_gram(matrix, out_ref, precision):
    columns = matrix.shape[1]
    place = 0
    for i in range(columns // GB):
        strip = dot(matrix[:, i * GB : i * GB + GB], matrix[:, i * GB :], 0, 0, precision)
        for j in range(columns // GB - i):
            out_ref[place * GB : place * GB + GB, :] = strip[:, j * GB : j * GB + GB]
            place += 1


def sketch_gram_kernel(parts_ref, out_ref):
    total = jnp.sum(parts_ref[...], axis=0)
    pack_gram(total, out_ref, HIGHEST)


def sketch_gram(parts):
    columns = parts.shape[2]
    return pl.pallas_call(
        sketch_gram_kernel,
        out_shape=jax.ShapeDtypeStruct((len(upper_blocks(columns)) * GB, GB), jnp.float32),
        in_specs=[VMEM],
        out_specs=VMEM,
        compiler_params=PARAMS,
        name="sketch_gram",
    )(parts)


def whiten_kernel(panel_ref, inverse_ref, white_ref, out_ref):
    rows = panel_ref.shape[0]
    for start in range(0, rows, 256):
        white_ref[start : start + 256, :] = dot(
            panel_ref[start : start + 256, :], inverse_ref[...], 1, 1
        ).astype(jnp.bfloat16)
    pack_gram(white_ref[...], out_ref, None)


def whiten(panel, inverse):
    columns = panel.shape[1]
    return pl.pallas_call(
        whiten_kernel,
        out_shape=(
            jax.ShapeDtypeStruct(panel.shape, jnp.bfloat16),
            jax.ShapeDtypeStruct((len(upper_blocks(columns)) * GB, GB), jnp.float32),
        ),
        in_specs=[VMEM] * 2,
        out_specs=(VMEM, VMEM),
        compiler_params=PARAMS,
        name="whiten",
    )(panel, inverse)


def factor_block(block):
    row = lax.broadcasted_iota(jnp.int32, (NB, NB), 0)
    column = lax.broadcasted_iota(jnp.int32, (NB, NB), 1)
    both = jnp.concatenate([block, (row == column).astype(jnp.float32)], axis=1)
    count = NB // 8
    work = [both[8 * u : 8 * u + 8, :] for u in range(count)]
    sub = lax.broadcasted_iota(jnp.int32, (8, 128), 0)
    done = [None] * count
    for j in range(NB):
        t, k = divmod(j, 8)
        lanes = {u: jnp.broadcast_to(work[u][:, j : j + 1], (8, 128)) for u in range(t, count)}
        pivot_row = jnp.broadcast_to(work[t][k : k + 1, :], (8, 128))
        pivot = jnp.broadcast_to(lanes[t][k : k + 1, :], (8, 128))
        scaled = pivot_row * (1.0 / pivot)
        final = pivot_row * lax.rsqrt(pivot)
        done[t] = final if k == 0 else jnp.where(sub == k, final, done[t])
        if k < 7:
            work[t] = jnp.where(sub > k, work[t] - lanes[t] * scaled, work[t])
        for u in range(t + 1, count):
            work[u] = work[u] - lanes[u] * scaled
    return jnp.concatenate(done, axis=0)


def factor_kernel(scale, packed_ref, factor_ref, inverse_ref, work):
    order = work.shape[0]
    for place, (i, j) in enumerate(upper_blocks(order)):
        block = packed_ref[place * GB : place * GB + GB, :] * scale
        work[i * GB : i * GB + GB, j * GB : j * GB + GB] = block
        if i != j:
            work[j * GB : j * GB + GB, i * GB : i * GB + GB] = block.T
    row = lax.broadcasted_iota(jnp.int32, (NB, NB), 0)
    column = lax.broadcasted_iota(jnp.int32, (NB, NB), 1)
    wide = lax.broadcasted_iota(jnp.int32, (NB, order), 1)
    for end in range(NB, order + 1, NB):
        own = slice(end - NB, end)
        rest = slice(end, order)
        both = factor_block(work[own, own])
        diagonal = jnp.where(row <= column, both[:, :NB], 0.0)
        inverse = both[:, NB:]
        if end < order:
            left = dot(work[rest, own], inverse, 1, 1, HIGHEST)
        work[own, own] = (row == column).astype(jnp.float32)
        strip = dot(inverse, work[own, :], 1, 0, HIGHEST)
        inverse_ref[own, :] = jnp.where(wide < end, strip, 0.0).astype(jnp.bfloat16)
        factor_ref[own, :] = jnp.where(wide >= end, strip, 0.0)
        factor_ref[own, own] = diagonal
        if end < order:
            work[rest, own] = jnp.zeros((order - end, NB), jnp.float32)
            work[rest, :] = work[rest, :] - dot(left, strip, 1, 0, HIGHEST)


def factor(packed, order, scale):
    return pl.pallas_call(
        functools.partial(factor_kernel, scale),
        out_shape=(
            jax.ShapeDtypeStruct((order, order), jnp.float32),
            jax.ShapeDtypeStruct((order, order), jnp.bfloat16),
        ),
        in_specs=[VMEM],
        out_specs=(VMEM, VMEM),
        scratch_shapes=[pltpu.VMEM((order, order), jnp.float32)],
        compiler_params=PARAMS,
        name="factor",
    )(packed)


def sum_all(packed):
    count = lax.axis_size(AXES)
    chunk = packed.shape[0] // count
    parts = packed.reshape(count, chunk // 2, 2, GB)
    parts = lax.all_to_all(parts, AXES, 0, 0, tiled=True)
    total = jnp.sum(parts, axis=0, keepdims=True)
    parts = jnp.broadcast_to(total, parts.shape)
    parts = lax.all_to_all(parts, AXES, 0, 0, tiled=True)
    return parts.reshape(packed.shape)


def parity(value):
    for shift in (8, 4, 2, 1):
        value = jnp.bitwise_xor(value, jnp.right_shift(value, shift))
    return jnp.bitwise_and(value, 1)


def on_device(panel, signs, sample_rows):
    core = lax.axis_index("c")
    n_had = lax.axis_size("z") * lax.axis_size("c")
    n_blk = lax.axis_size("x") * lax.axis_size("y")
    my_group = lax.axis_index(("z", "c"))
    rows_dev, columns = panel.shape
    sketch_count = sample_rows.shape[1]
    half = sketch_count // 2
    owners = sample_rows // rows_dev
    offsets = sample_rows % rows_dev
    codes = offsets + 65536 * parity(jnp.bitwise_and(owners, my_group))
    signs = signs.reshape(1, rows_dev)
    sent = lax.dynamic_slice_in_dim(codes, (1 - core) * half, half, 1)
    kept = lax.dynamic_slice_in_dim(codes, core * half, half, 1)
    other = lax.ppermute(sketch_rows(sent, signs, panel), "c", [(0, 1), (1, 0)])
    mine = sketch_rows(kept, signs, panel) + other
    chips = lax.axis_size(CHIPS)
    mine = mine.reshape(chips, half // chips, columns)
    parts = lax.all_to_all(mine, CHIPS, 0, 0, tiled=True)
    packed = sum_all(sketch_gram(parts))
    r_sketch, sketch_inverse = factor(
        packed, columns, 1.0 / (n_had * LH * sketch_count * n_blk)
    )
    whitened, packed = whiten(panel, sketch_inverse)
    packed = sum_all(packed)
    r_gram, gram_inverse = factor(packed, columns, 1.0 / (rows_dev * n_had * n_blk))
    q_panel = dot(whitened, gram_inverse, 1, 1).astype(jnp.bfloat16)
    return (q_panel, r_sketch, r_gram)


def solution(mesh):
    devices = mesh.devices.reshape(4, 2, 4, 4)
    split = Mesh(devices, AXES)
    placed = (P(AXES, None), P(AXES), P(("x", "y"), None))
    return jax.shard_map(
        on_device,
        mesh=split,
        in_specs=placed,
        out_specs=(P(AXES, None), P(), P()),
        check_vma=False,
    )
```

time: 1260 us -> 300 us (0.24)
  local copies, waits for them, and re-layouts: 708 us -> 3.96 us
  waiting for transfers between devices: 302 us -> 1.38 us
  other arithmetic: 175 us -> 1.76 us
  Pallas kernels: 0 us -> 170 us
  blocking collectives: 0 us -> 118 us
  matrix products: 49 us -> 2.6 us
  between operations: 21 us -> 0.94 us
    reshape x32 -> x0, local copies, waits for them, and re-layouts: 635 us -> none  [lower_inverse(): tiles = lower.reshape(count, 2 * width, count, 2 * width)]
    psum x2 -> x0, waiting for transfers between devices: 302 us -> none  [the longest x1 157 us: on_device(): sketch = lax.psum(partial_sketch, ('had', 'blk'))]
    pallas_call x0 -> x6, Pallas kernels: none -> 170 us  [the longest x2 162 us: factor(): pl.pallas_call(functools.partial(factor_kernel, scale), out_shape=(jax.Sh...]
    another operation x29 -> x0, other arithmetic: 158 us -> none  [upper_factor(): return jnp.linalg.cholesky(matrix).T]
    all_to_all x0 -> x5, blocking collectives: none -> 118 us  [the longest x4 79 us: sum_all(): parts = lax.all_to_all(parts, AXES, 0, 0, tiled=True)]
    gather x19 -> x0, local copies, waits for them, and re-layouts: 61.2 us -> none  [the longest x16 40.2 us: lower_inverse(): diag_tiles = jnp.moveaxis(jnp.diagonal(tiles, axis1=0, axis2=2), -1, 0)]
    dot_general x37 -> x1, matrix products: 41.7 us -> 2.6 us  [dot(): lax.dot_general(first, second, (((first_dim,), (second_dim,)), ((), ())),...]
  transfers between devices with their start and end apart: 2 -> 1, of which waited for: 2 -> 1; matrix products, arithmetic and copies ran while one was open for 0% -> 0% of each run, Pallas kernels for 0% -> 1%
where the time goes in v1:
time: 300 us
  Pallas kernels  170 us (57%)
  blocking collectives  118 us (39%)
  local copies, waits for them, and re-layouts  3.96 us (1%)
    pallas_call x2, Pallas kernels, factor(): pl.pallas_call(functools.partial(factor_kernel, scale), out_shape=(jax.Sh...  162 us
    all_to_all x4, blocking collectives, sum_all(): parts = lax.all_to_all(parts, AXES, 0, 0, tiled=True)  79 us
    all_to_all x1, blocking collectives, on_device(): parts = lax.all_to_all(mine, CHIPS, 0, 0, tiled=True)  39.1 us
  transfers between devices with their start and end apart: 1, of which 1 were waited for; matrix products, arithmetic and copies ran while one was open for 0% of the time, Pallas kernels for 1%

profile of v1, /device:TPU:1, one launch (start us, length us, event | category | flops | bytes accessed | tf_op | source)
XLA Modules:
  0.0 300.1 jit_solution(15336473853627325033)
XLA Ops:
  0.6 0.8 fusion
  1.4 0.0 copy-start
  1.5 1.6 copy-done
  3.0 0.0 copy-start.2
  3.0 0.7 copy-done.2
  3.7 0.0 copy-start.1
  3.7 0.0 copy-start.3
  3.7 2.4 sketch_rows.3
  6.1 1.5 collective-permute-start
  7.6 0.0 copy-done.1
  7.6 0.0 copy-done.3
  7.7 2.4 sketch_rows.2
  10.1 1.4 collective-permute-done
  11.4 0.5 add.27
  11.9 39.1 %all_to_all.25.parts_ref = f32[64,16,512]{2,1,0:T(8,128)S(1)} all-to-all(f32[64,16,512]{2,1,0:T(8,128)S(1)} %bitcast.14), channel_id=1, replica_groups=mesh['z'=4,'c'=2,'x'=4,'y'=4] {'z','x','y'}, dimensions={0} | all-to-all | bytes 4194304 | tf_op jit(solution)/shard_map/all_to_all | solution.py:231
  51.0 0.8 sketch_gram.1
  51.8 21.9 %all_to_all.26 = f32[128,5,2,128]{3,2,1,0:T(2,128)S(1)} all-to-all(f32[128,5,2,128]{3,2,1,0:T(2,128)S(1)} %bitcast.10), channel_id=1, replica_groups=mesh['z'=4,'c'=2,'x'=4,'y'=4] {'z','c','x','y'}, dimensions={0} | all-to-all | bytes 1310720 | tf_op jit(solution)/shard_map/all_to_all | solution.py:200
  73.7 0.2 reduce_sum.18
  73.9 0.2 broadcast_in_dim.4
  74.1 19.0 %all_to_all.27 = f32[128,5,2,128]{3,2,1,0:T(2,128)S(1)} all-to-all(f32[128,5,2,128]{3,2,1,0:T(2,128)S(1)} %broadcast_in_dim.4), channel_id=1, replica_groups=mesh['z'=4,'c'=2,'x'=4,'y'=4] {'z','c','x','y'}, dimensions={0} | all-to-all | bytes 1310720 | tf_op jit(solution)/shard_map/all_to_all | solution.py:203
  93.1 87.0 %factor.2 = (f32[512,512]{1,0:T(8,128)}, bf16[512,512]{1,0:T(8,128)(2,1)S(1)}) custom-call(f32[1280,128]{1,0:T(8,128)S(1)} %bitcast.8), custom_call_target="tpu_custom_call" | custom-call | tf_op jit(solution)/shard_map/factor/pallas_call | solution.py:182
  180.2 2.1 whiten.1
  182.3 0.0 copy-start.4
  182.3 1.3 copy-done.4
  183.6 0.0 copy-start.5
  183.6 19.1 %all_to_all.28 = f32[128,5,2,128]{3,2,1,0:T(2,128)S(1)} all-to-all(f32[128,5,2,128]{3,2,1,0:T(2,128)S(1)} %bitcast.11), channel_id=1, replica_groups=mesh['z'=4,'c'=2,'x'=4,'y'=4] {'z','c','x','y'}, dimensions={0} | all-to-all | bytes 1310720 | tf_op jit(solution)/shard_map/all_to_all | solution.py:200
  202.7 0.2 reduce_sum.19
  202.9 0.2 broadcast_in_dim.5
  203.1 19.0 %all_to_all.29 = f32[128,5,2,128]{3,2,1,0:T(2,128)S(1)} all-to-all(f32[128,5,2,128]{3,2,1,0:T(2,128)S(1)} %broadcast_in_dim.5), channel_id=1, replica_groups=mesh['z'=4,'c'=2,'x'=4,'y'=4] {'z','c','x','y'}, dimensions={0} | all-to-all | bytes 1310720 | tf_op jit(solution)/shard_map/all_to_all | solution.py:203
  222.1 75.1 %factor.3 = (f32[512,512]{1,0:T(8,128)}, bf16[512,512]{1,0:T(8,128)(2,1)S(1)}) custom-call(f32[1280,128]{1,0:T(8,128)S(1)} %bitcast.9), custom_call_target="tpu_custom_call" | custom-call | tf_op jit(solution)/shard_map/factor/pallas_call | solution.py:182
  297.2 0.0 copy-done.5
  297.2 2.6 convolution_convert_fusion
  (1 shorter events, 0.0 us)
Async XLA Ops:
  1.4 1.6 copy-start
  3.0 0.7 copy-start.2
  3.7 3.9 %copy-start.1 = (bf16[2048,512]{1,0:T(8,128)(2,1)S(1)}, bf16[2048,512]{1,0:T(8,128)(2,1)}, u32[]{:S(2)}) copy-start(bf16[2048,512]{1,0:T(8,128)(2,1)} %panel_ref.5) | copy-start | bytes 6291460
  3.7 3.9 %copy-start.3 = (s32[2048]{0:T(1024)S(1)}, s32[2048]{0:T(1024)}, u32[]{:S(2)}) copy-start(s32[2048]{0:T(1024)} %param.4) | copy-start | bytes 24580
  6.1 5.3 %collective-permute-start = (f32[1024,512]{1,0:T(8,128)S(1)}, f32[1024,512]{1,0:T(8,128)S(1)}, u32[]{:S(2)}, u32[]{:S(2)}) collective-permute-start(f32[1024,512]{1,0:T(8,128)S(1)} %sketch_rows.3), channel_id=1, source_target_pairs={{0,16},{16,0},{1,17},{17,1},{2,18},{18,2},{3,19},{19,3},{4,20},{20... | collective-permute-start | bytes 6291464 | tf_op jit(solution)/shard_map/ppermute | solution.py:227
  182.3 1.3 copy-start.4
  183.6 113.6 %copy-start.5 = (bf16[2048,512]{1,0:T(8,128)(2,1)S(1)}, bf16[2048,512]{1,0:T(8,128)(2,1)}, u32[]{:S(2)}) copy-start(bf16[2048,512]{1,0:T(8,128)(2,1)} %copy-done.4) | copy-start | bytes 6291460

commit v2 on v1

--- a/solution.py
+++ b/solution.py
@@ -127,6 +127,10 @@
     )(panel, inverse)
 
 
+def spread_row(tile, k):
+    return jnp.broadcast_to(tile[k : k + 1, :], tile.shape)
+
+
 def factor_block(block):
     row = lax.broadcasted_iota(jnp.int32, (NB, NB), 0)
     column = lax.broadcasted_iota(jnp.int32, (NB, NB), 1)
@@ -134,19 +138,30 @@
     count = NB // 8
     work = [both[8 * u : 8 * u + 8, :] for u in range(count)]
     sub = lax.broadcasted_iota(jnp.int32, (8, 128), 0)
-    done = [None] * count
-    for j in range(NB):
-        t, k = divmod(j, 8)
-        lanes = {u: jnp.broadcast_to(work[u][:, j : j + 1], (8, 128)) for u in range(t, count)}
-        pivot_row = jnp.broadcast_to(work[t][k : k + 1, :], (8, 128))
-        pivot = jnp.broadcast_to(lanes[t][k : k + 1, :], (8, 128))
-        scaled = pivot_row * (1.0 / pivot)
-        final = pivot_row * lax.rsqrt(pivot)
-        done[t] = final if k == 0 else jnp.where(sub == k, final, done[t])
-        if k < 7:
-            work[t] = jnp.where(sub > k, work[t] - lanes[t] * scaled, work[t])
-        for u in range(t + 1, count):
-            work[u] = work[u] - lanes[u] * scaled
+    done = []
+    for t in range(count):
+        first = 8 * t
+        lanes = {
+            u: [jnp.broadcast_to(work[u][:, first + c : first + c + 1], (8, 128)) for c in range(8)]
+            for u in range(t, count)
+        }
+        pivots = None
+        for k in range(8):
+            pivot = spread_row(lanes[t][k], k)
+            pivots = pivot if k == 0 else jnp.where(sub == k, pivot, pivots)
+            inverse = 1.0 / pivot
+            across = {c: spread_row(lanes[t][c], k) for c in range(k + 1, 8)}
+            pivot_row = spread_row(work[t], k)
+            for u in range(t, count):
+                if u == t and k == 7:
+                    continue
+                ratio = lanes[u][k] * inverse
+                if u == t:
+                    ratio = jnp.where(sub > k, ratio, 0.0)
+                for c in range(k + 1, 8):
+                    lanes[u][c] = lanes[u][c] - ratio * across[c]
+                work[u] = work[u] - ratio * pivot_row
+        done.append(work[t] * lax.rsqrt(pivots))
     return jnp.concatenate(done, axis=0)
 
 

time: 300 us -> 195 us (0.65)
  Pallas kernels: 170 us -> 64.1 us
    pallas_call x2, Pallas kernels: 162 us -> 56.5 us  [factor(): pl.pallas_call(functools.partial(factor_kernel, scale), out_shape=(jax.Sh...]
where the time goes in v2:
time: 195 us; the launch traced here: 194 us
  blocking collectives  118 us (61%)
  Pallas kernels  64.1 us (33%)
  local copies, waits for them, and re-layouts  3.96 us (2%)
  matrix products  2.6 us (1%)
    all_to_all x4, blocking collectives, sum_all(): parts = lax.all_to_all(parts, AXES, 0, 0, tiled=True)  79 us
    pallas_call x2, Pallas kernels, factor(): pl.pallas_call(functools.partial(factor_kernel, scale), out_shape=(jax.Sh...  56.5 us
    all_to_all x1, blocking collectives, on_device(): parts = lax.all_to_all(mine, CHIPS, 0, 0, tiled=True)  39.1 us
    pallas_call x2, Pallas kernels, sketch_rows(): pl.pallas_call(sketch_kernel, out_shape=jax.ShapeDtypeStruct((codes.shape...  4.79 us
  transfers between devices with their start and end apart: 1, of which 1 were waited for; matrix products, arithmetic and copies ran while one was open for 0% of the time, Pallas kernels for 1%

profile of v2, /device:TPU:1, one launch (start us, length us, event | category | flops | bytes accessed | tf_op | source)
XLA Modules:
  0.0 194.4 jit_solution(12425087459412574916)
XLA Ops:
  0.6 0.8 fusion
  1.4 0.0 copy-start
  1.5 1.6 copy-done
  3.0 0.0 copy-start.2
  3.0 0.7 copy-done.2
  3.7 0.0 copy-start.1
  3.7 0.0 copy-start.3
  3.7 2.4 %sketch_rows.3 = f32[1024,512]{1,0:T(8,128)S(1)} custom-call(s32[1,1024]{1,0:T(1,128)S(1)} %get-tuple-element.15.codes_ref, s32[1,2048]{1,0:T(1,128)S(1)} %bitcast.12, bf16[2048,512]{1,0:T(8,128)(2,1)S(1)} %copy-done), custom_call_target="tpu_custom_call" | custom-call | tf_op jit(solution)/shard_map/sketch_rows/pallas_call | solution.py:69
  6.1 1.5 collective-permute-start
  7.6 0.0 copy-done.1
  7.6 0.0 copy-done.3
  7.7 2.4 %sketch_rows.2 = f32[1024,512]{1,0:T(8,128)S(1)} custom-call(s32[1,1024]{1,0:T(1,128)S(1)} %get-tuple-element.16.codes_ref, s32[1,2048]{1,0:T(1,128)S(1)} %bitcast.13, bf16[2048,512]{1,0:T(8,128)(2,1)S(1)} %copy-done.1), custom_call_target="tpu_custom_call" | custom-call | tf_op jit(solution)/shard_map/sketch_rows/pallas_call | solution.py:69
  10.1 1.4 collective-permute-done
  11.4 0.5 add.27
  11.9 39.1 %all_to_all.25.parts_ref = f32[64,16,512]{2,1,0:T(8,128)S(1)} all-to-all(f32[64,16,512]{2,1,0:T(8,128)S(1)} %bitcast.14), channel_id=1, replica_groups=mesh['z'=4,'c'=2,'x'=4,'y'=4] {'z','x','y'}, dimensions={0} | all-to-all | bytes 4194304 | tf_op jit(solution)/shard_map/all_to_all | solution.py:246
  51.0 0.8 sketch_gram.1
  51.8 21.9 %all_to_all.26 = f32[128,5,2,128]{3,2,1,0:T(2,128)S(1)} all-to-all(f32[128,5,2,128]{3,2,1,0:T(2,128)S(1)} %bitcast.10), channel_id=1, replica_groups=mesh['z'=4,'c'=2,'x'=4,'y'=4] {'z','c','x','y'}, dimensions={0} | all-to-all | bytes 1310720 | tf_op jit(solution)/shard_map/all_to_all | solution.py:215
  73.7 0.2 reduce_sum.18
  73.9 0.2 broadcast_in_dim.4
  74.1 19.0 %all_to_all.27 = f32[128,5,2,128]{3,2,1,0:T(2,128)S(1)} all-to-all(f32[128,5,2,128]{3,2,1,0:T(2,128)S(1)} %broadcast_in_dim.4), channel_id=1, replica_groups=mesh['z'=4,'c'=2,'x'=4,'y'=4] {'z','c','x','y'}, dimensions={0} | all-to-all | bytes 1310720 | tf_op jit(solution)/shard_map/all_to_all | solution.py:218
  93.1 34.2 %factor.2 = (f32[512,512]{1,0:T(8,128)}, bf16[512,512]{1,0:T(8,128)(2,1)S(1)}) custom-call(f32[1280,128]{1,0:T(8,128)S(1)} %bitcast.8), custom_call_target="tpu_custom_call" | custom-call | tf_op jit(solution)/shard_map/factor/pallas_call | solution.py:197
  127.3 2.1 %whiten.1 = (bf16[2048,512]{1,0:T(8,128)(2,1)S(1)}, f32[1280,128]{1,0:T(8,128)S(1)}) custom-call(bf16[2048,512]{1,0:T(8,128)(2,1)S(1)} %copy-done.1, bf16[512,512]{1,0:T(8,128)(2,1)S(1)} %get-tuple-element.9.inverse_ref), custom_call_target="tpu_custom_call" | custom-call | tf_op jit(solution)/shard_map/whiten/pallas_call | solution.py:117
  129.4 0.0 copy-start.4
  129.5 1.3 copy-done.4
  130.8 0.0 copy-start.5
  130.8 19.1 %all_to_all.28 = f32[128,5,2,128]{3,2,1,0:T(2,128)S(1)} all-to-all(f32[128,5,2,128]{3,2,1,0:T(2,128)S(1)} %bitcast.11), channel_id=1, replica_groups=mesh['z'=4,'c'=2,'x'=4,'y'=4] {'z','c','x','y'}, dimensions={0} | all-to-all | bytes 1310720 | tf_op jit(solution)/shard_map/all_to_all | solution.py:215
  149.8 0.2 reduce_sum.19
  150.1 0.2 broadcast_in_dim.5
  150.3 19.0 %all_to_all.29 = f32[128,5,2,128]{3,2,1,0:T(2,128)S(1)} all-to-all(f32[128,5,2,128]{3,2,1,0:T(2,128)S(1)} %broadcast_in_dim.5), channel_id=1, replica_groups=mesh['z'=4,'c'=2,'x'=4,'y'=4] {'z','c','x','y'}, dimensions={0} | all-to-all | bytes 1310720 | tf_op jit(solution)/shard_map/all_to_all | solution.py:218
  169.3 22.3 %factor.3 = (f32[512,512]{1,0:T(8,128)}, bf16[512,512]{1,0:T(8,128)(2,1)S(1)}) custom-call(f32[1280,128]{1,0:T(8,128)S(1)} %bitcast.9), custom_call_target="tpu_custom_call" | custom-call | tf_op jit(solution)/shard_map/factor/pallas_call | solution.py:197
  191.6 0.0 copy-done.5
  191.6 2.6 %convolution_convert_fusion = bf16[2048,512]{1,0:T(8,128)(2,1)} fusion(bf16[2048,512]{1,0:T(8,128)(2,1)S(1)} %copy-done.5, bf16[512,512]{1,0:T(8,128)(2,1)S(1)} %get-tuple-element.12), kind=kOutput, calls=%fused_computation | convolution fusion | flops 1074790400 | bytes 4718592 | tf_op jit(solution)/shard_map/dot_general | solution.py:21
  (1 shorter events, 0.0 us)
Async XLA Ops:
  1.4 1.6 copy-start
  3.0 0.7 copy-start.2
  3.7 3.9 %copy-start.1 = (bf16[2048,512]{1,0:T(8,128)(2,1)S(1)}, bf16[2048,512]{1,0:T(8,128)(2,1)}, u32[]{:S(2)}) copy-start(bf16[2048,512]{1,0:T(8,128)(2,1)} %panel_ref.5) | copy-start | bytes 6291460
  3.7 3.9 %copy-start.3 = (s32[2048]{0:T(1024)S(1)}, s32[2048]{0:T(1024)}, u32[]{:S(2)}) copy-start(s32[2048]{0:T(1024)} %param.4) | copy-start | bytes 24580
  6.1 5.3 %collective-permute-start = (f32[1024,512]{1,0:T(8,128)S(1)}, f32[1024,512]{1,0:T(8,128)S(1)}, u32[]{:S(2)}, u32[]{:S(2)}) collective-permute-start(f32[1024,512]{1,0:T(8,128)S(1)} %sketch_rows.3), channel_id=1, source_target_pairs={{0,16},{16,0},{1,17},{17,1},{2,18},{18,2},{3,19},{19,3},{4,20},{20... | collective-permute-start | bytes 6291464 | tf_op jit(solution)/shard_map/ppermute | solution.py:242
  129.4 1.3 copy-start.4
  130.8 60.8 %copy-start.5 = (bf16[2048,512]{1,0:T(8,128)(2,1)S(1)}, bf16[2048,512]{1,0:T(8,128)(2,1)}, u32[]{:S(2)}) copy-start(bf16[2048,512]{1,0:T(8,128)(2,1)} %copy-done.4) | copy-start | bytes 6291460
